TPU v7x, 32 devices: a whole 2x2x4 slice. The times are simulated.
32 devices in a mesh: gr: 4 (over y, core), gc: 8 (over z, x).
Axes of the slice: x: 2, y: 2, z: 4, core: 2. Of those that a mesh axis runs over, the one named last changes fastest.
Arguments:
- features: bfloat16 [4096, 1024], P(('gr', 'gc')), may hold values from -6 to 6
- weight: bfloat16 [1024, 1024], replicated, may hold values from -0.1875 to 0.1875
- cotangent: bfloat16 [4096, 1024], P(('gr', 'gc')), may hold values from -6 to 6
- block_values: bfloat16 [32, 4, 128, 128], P(('gr', 'gc')), as said below
- block_codes: int32 [32, 4], P(('gr', 'gc')), may hold values from 0 to 31, as said below
- block_count: int32 [32], P(('gr', 'gc')), may hold values from 1 to 4, as said below
Outputs:
- output: float32 [4096, 1024], P(('gr', 'gc'))
- input_grad: float32 [4096, 1024], P(('gr', 'gc'))
- weight_grad: float32 [1024, 1024], P('gc')
Inputs may be any that keep to these rules, and one draw needn't show every extreme that they name: `block_codes`: write code = row * 32 + column. In every slot, row lies in 0 to 0 and column is a block of a slice s + j * 8 with |j| <= 2 (same grid column, at most 2 grid rows away). The codes of the live slots of one slice differ from one another. Every diagonal block (block row equal to block column) is live. The live slots of a slice are its first block_count slots; the entries of later slots are not part of the adjacency. In every draw some slice has all 4 slots live. `block_values`: the adjacency is symmetric: a block is live exactly when its mirror block is, and its entries are the transpose of the mirror's.
All inputs are finite; a program needn't handle non-finite values.
Results may differ from a plain program's by a relative error of at most 0.0045.
Values may be sent and summed in bfloat16 or wider, within the bound.
A program may use at most 64 MiB of HBM per device.

v0:
```python
import jax
import jax.numpy as jnp
from jax import lax
from jax.sharding import PartitionSpec as P


def dense_tile(row_index, block_index, active, values, piece_blocks, row_blocks):
    block_size = values.shape[-1]
    select_col = (block_index[:, None] == jnp.arange(piece_blocks)[None, :]) & active[:, None]
    select_row = row_index[:, None] == jnp.arange(row_blocks)[None, :]
    tiled = jnp.einsum(
        "ka,km,kij->aimj",
        select_row.astype(jnp.bfloat16),
        select_col.astype(jnp.bfloat16),
        values,
        preferred_element_type=jnp.float32,
    )
    return tiled.astype(jnp.bfloat16).reshape(row_blocks * block_size, piece_blocks * block_size)


def aggregate(source, layout):
    row_index, block_index, active, values = layout
    node_rows = source.shape[0]
    block_size = values.shape[-1]
    row_blocks = node_rows // block_size
    portion = lax.all_gather(source, "gr", axis=0, tiled=True)
    tile = dense_tile(
        row_index, block_index, active, values, portion.shape[0] // block_size, row_blocks
    )
    return jnp.dot(tile, portion, preferred_element_type=jnp.float32)


def local(features, weight, cotangent, block_values, block_codes, block_count):
    node_rows = features.shape[0]
    block_size = block_values.shape[-1]
    row_blocks = node_rows // block_size
    grid_cols = lax.axis_size("gc")
    grid_rows = lax.axis_size("gr")
    all_blocks = row_blocks * grid_rows * grid_cols
    slot_codes = block_codes[0]
    row_index = slot_codes // all_blocks
    column_block = slot_codes % all_blocks
    block_index = column_block // row_blocks // grid_cols * row_blocks + column_block % row_blocks
    active = jnp.arange(slot_codes.shape[0]) < block_count[0]
    layout = (row_index, block_index, active, block_values[0])
    projected = jnp.dot(features, weight, preferred_element_type=jnp.float32).astype(jnp.bfloat16)
    summed = aggregate(projected, layout)
    sigmoid = jax.nn.sigmoid(summed)
    output = summed * sigmoid
    act_slope = (cotangent.astype(jnp.float32) * sigmoid * (1.0 + summed * (1.0 - sigmoid))).astype(
        jnp.bfloat16
    )
    back_grad = aggregate(act_slope, layout).astype(jnp.bfloat16)
    input_grad = lax.dot_general(
        back_grad, weight, (((1,), (1,)), ((), ())), preferred_element_type=jnp.float32
    )
    grad_scale = (node_rows * grid_rows * grid_cols) ** (-0.5)
    partial_grad = (
        lax.dot_general(
            features, back_grad, (((0,), (0,)), ((), ())), preferred_element_type=jnp.float32
        )
        * grad_scale
    )
    row_share = lax.psum_scatter(partial_grad, "gc", scatter_dimension=0, tiled=True)
    weight_grad = lax.psum(row_share, "gr")
    return (output, input_grad, weight_grad)


def solution(mesh):
    in_specs = (
        P(("gr", "gc"), None),
        P(),
        P(("gr", "gc"), None),
        P(("gr", "gc"), None, None, None),
        P(("gr", "gc"), None),
        P(("gr", "gc")),
    )
    out_specs = (P(("gr", "gc"), None), P(("gr", "gc"), None), P("gc", None))
    return jax.shard_map(local, mesh=mesh, in_specs=in_specs, out_specs=out_specs, check_vma=False)
```

profile of v0, /device:TPU:1, one launch (start us, length us, event | category | flops | bytes accessed | tf_op | source)
XLA Modules:
  0.0 184.6 jit_solution(14487322982715928400)
XLA Ops:
  7.2 0.0 copy-start
  7.2 0.0 copy-start.2
  7.2 0.0 copy-start.4
  7.2 0.0 copy-start.3
  7.2 0.0 all-gather.3.cloned.1.call-start
  7.3 1.5 copy-done
  8.8 2.1 %convolution_convert_fusion.1 = bf16[128,1024]{1,0:T(8,128)(2,1)} fusion(bf16[128,1024]{1,0:T(8,128)(2,1)} %param.6, bf16[1024,1024]{1,0:T(8,128)(2,1)S(1)} %copy-done), kind=kOutput, calls=%fused_computation.2 | convolution fusion | flops 268566528 | bytes 2621440 | tf_op jit(solution)/shard_map/dot_general | solution.py:46
  10.9 0.0 all-gather.3.cloned.1.call-update
  10.9 0.0 all-gather.5.cloned.1.call-start
  11.6 0.0 copy-done.2
  11.6 0.0 copy-done.4
  11.6 0.2 convolution_convert_fusion.2
  11.9 18.4 %all-gather.3.cloned.1.call-done = bf16[512,1024]{1,0:T(8,128)(2,1)} async-done(((bf16[128,1024]{1,0:T(8,128)(2,1)}), bf16[512,1024]{1,0:T(8,128)(2,1)}) %all-gather.3.cloned.1.call-update) | async-done | bytes 1048592 | tf_op jit(solution)/shard_map/all_gather | solution.py:26
  30.2 0.0 copy-done.3
  30.3 0.0 copy-start.1
  30.3 2.6 %multiply_convert_fusion = (bf16[128,1024]{1,0:T(8,128)(2,1)}, f32[128,1024]{1,0:T(8,128)}) fusion(bf16[128,1024]{1,0:T(8,128)(2,1)S(1)} %copy-done.3, bf16[512,1024]{1,0:T(8,128)(2,1)} %all-gather.3.cloned.1.call-done, bf16[16,8,4,128]{3,2,1,0:T(4,128)(2,1)S(1)} %bitcast.45), kind=kOutput, calls=%fused_computation.4 | convolution fusion | flops 135659520 | bytes 2228224 | tf_op jit(solution)/shard_map/dot_general | solution.py:30
  32.8 0.0 all-gather.5.cloned.1.call-update
  32.9 0.0 reduce-scatter.2.cloned.1.call-start
  32.9 16.8 %all-gather.5.cloned.1.call-done = bf16[512,1024]{1,0:T(8,128)(2,1)} async-done(((bf16[128,1024]{1,0:T(8,128)(2,1)}), bf16[512,1024]{1,0:T(8,128)(2,1)}) %all-gather.5.cloned.1.call-update) | async-done | bytes 1048592 | tf_op jit(solution)/shard_map/all_gather | solution.py:26
  49.8 1.5 convolution_convert_fusion
  51.3 0.0 copy-done.1
  51.3 2.7 %multiply_bitcast_fusion = f32[1024,1024]{0,1:T(8,128)} fusion(bf16[128,1024]{1,0:T(8,128)(2,1)S(1)} %convolution_convert_fusion, bf16[128,1024]{1,0:T(8,128)(2,1)S(1)} %copy-done.1), kind=kOutput, calls=%fused_computation | convolution fusion | flops 269484032 | bytes 4718592 | tf_op jit(solution)/shard_map/dot_general | solution.py:59
  54.0 0.0 reduce-scatter.2.cloned.1.call-update
  54.0 0.0 all-reduce.2.cloned.1.call-start
  54.1 88.2 %reduce-scatter.2.cloned.1.call-done = f32[128,1024]{0,1:T(8,128)} async-done(((f32[1024,1024]{0,1:T(8,128)}), f32[128,1024]{0,1:T(8,128)}) %reduce-scatter.2.cloned.1.call-update) | async-done | bytes 524304 | tf_op jit(solution)/shard_map/reduce_scatter | solution.py:64
  142.3 0.0 all-reduce.2.cloned.1.call-update
  142.3 1.6 fusion.16
  143.9 32.1 %all-reduce.2.cloned.1.call-done = f32[128,1024]{0,1:T(8,128)} async-done(((f32[128,1024]{0,1:T(8,128)}), f32[128,1024]{0,1:T(8,128)}) %all-reduce.2.cloned.1.call-update) | async-done | bytes 524304 | tf_op jit(solution)/shard_map/psum | solution.py:65
  176.0 2.0 %copy.10 = f32[128,1024]{1,0:T(8,128)} copy(f32[128,1024]{0,1:T(8,128)} %all-reduce.2.cloned.1.call-done) | data formatting | bytes 1048576
  (2 shorter events, 0.0 us)
Async XLA Ops:
  7.2 1.6 copy-start
  7.2 4.4 %copy-start.2 = (s32[1,4]{1,0:T(1,128)S(1)}, s32[1,4]{1,0:T(1,128)}, u32[]{:S(2)}) copy-start(s32[1,4]{1,0:T(1,128)} %param.10) | copy-start | bytes 52
  7.2 4.4 %copy-start.4 = (bf16[1,4,128,128]{3,2,1,0:T(8,128)(2,1)S(1)}, bf16[1,4,128,128]{3,2,1,0:T(8,128)(2,1)}, u32[]{:S(2)}) copy-start(bf16[1,4,128,128]{3,2,1,0:T(8,128)(2,1)} %param.9) | copy-start | bytes 393220
  7.2 23.1 %copy-start.3 = (bf16[128,1024]{1,0:T(8,128)(2,1)S(1)}, bf16[128,1024]{1,0:T(8,128)(2,1)}, u32[]{:S(2)}) copy-start(bf16[128,1024]{1,0:T(8,128)(2,1)} %param.8) | copy-start | bytes 786436
  7.2 23.0 %all-gather.3.cloned.1.call-start = ((), (), s32[]{:S(2)}) async-start(), calls=%async_computation.1 | async-start | bytes 1310720 | tf_op jit(solution)/shard_map/all_gather | solution.py:26
  10.9 38.9 %all-gather.5.cloned.1.call-start = ((), (), s32[]{:S(2)}) async-start(), calls=%async_computation.2 | async-start | bytes 1310720 | tf_op jit(solution)/shard_map/all_gather | solution.py:26
  30.3 21.0 %copy-start.1 = (bf16[128,1024]{1,0:T(8,128)(2,1)S(1)}, bf16[128,1024]{1,0:T(8,128)(2,1)}, u32[]{:S(2)}) copy-start(bf16[128,1024]{1,0:T(8,128)(2,1)} %param.6) | copy-start | bytes 786436
  32.9 109.4 %reduce-scatter.2.cloned.1.call-start = ((), (), s32[]{:S(2)}) async-start(), calls=%async_computation.3 | async-start | bytes 4718592 | tf_op jit(solution)/shard_map/reduce_scatter | solution.py:64
  54.0 122.0 %all-reduce.2.cloned.1.call-start = ((), (), s32[]{:S(2)}) async-start(), calls=%async_computation.4 | async-start | bytes 1048576 | tf_op jit(solution)/shard_map/psum | solution.py:65
Sparse Core Ops, SparseCore 0:
  11.0 19.1 all-gather.2
  33.0 16.7 all-gather.4
  54.1 88.1 reduce-scatter.1
  144.6 31.3 all-reduce.1
where the time goes:
time: 187 us; the launch traced here: 185 us
  waiting for transfers between devices  156 us (83%)
  between operations  14.5 us (8%)
  matrix products  10.7 us (6%)
  local copies, waits for them, and re-layouts  3.56 us (2%)
    reduce_scatter x1, waiting for transfers between devices, local(): lax.psum_scatter(partial_grad, 'gc', scatter_dimension=0, tiled=True)  88.2 us
    all_gather x2, waiting for transfers between devices, aggregate(): portion = lax.all_gather(source, 'gr', axis=0, tiled=True)  35.2 us
    psum x1, waiting for transfers between devices, local(): weight_grad = lax.psum(row_share, 'gr')  32.1 us
    dot_general x2, matrix products, aggregate(): return jnp.dot(tile, portion, preferred_element_type=jnp.float32)  4.13 us
  transfers between devices with their start and end apart: 4, of which 4 were waited for; matrix products, arithmetic and copies ran while one was open for 1% of the time, Pallas kernels for 0%

commit v1 on v0

--- a/solution.py
+++ b/solution.py
@@ -1,7 +1,13 @@
+import functools
+
 import jax
 import jax.numpy as jnp
 from jax import lax
+from jax.experimental import pallas as pl
+from jax.experimental.pallas import tpu as pltpu
 from jax.sharding import PartitionSpec as P
+
+MESH = pl.DeviceIdType.MESH
 
 
 def dense_tile(row_index, block_index, active, values, piece_blocks, row_blocks):
@@ -30,7 +36,7 @@
     return jnp.dot(tile, portion, preferred_element_type=jnp.float32)
 
 
-def local(features, weight, cotangent, block_values, block_codes, block_count):
+def by_rows(features, weight, cotangent, block_values, block_codes, block_count):
     node_rows = features.shape[0]
     block_size = block_values.shape[-1]
     row_blocks = node_rows // block_size
@@ -66,6 +72,258 @@
     return (output, input_grad, weight_grad)
 
 
+def layer_kernel(
+    n_gr, n_gc, scale,
+    feat, wt, cot, vals, codes, count,
+    out_o, ig_o, wg_o,
+    fa, ft, wq, wv, vv, aa, pj, cq, ob, bq, br, iv, xs, xr, ac, zs, zr, wb,
+    loc, f_s, f_r, g_s, g_r, a_s, a_r, b_s, b_r, c_s, c_r, o_s, o_r, k_s, k_r,
+    x_s, x_r, z_s, z_r, w_s, w_r,
+):
+    rows, width = feat.shape
+    share = width // n_gr
+    chips, n_z = n_gr // 2, n_gc // 2
+    r, g = lax.axis_index("gr"), lax.axis_index("gc")
+    chip, core = r // 2, r % 2
+    z, x = g // 2, g % 2
+    mate = chip * 2 + 1 - core
+    f32, bf16 = jnp.float32, jnp.bfloat16
+
+    def rowsof(s):
+        return pl.ds(pl.multiple_of(s * rows, rows), rows)
+
+    def cols(s):
+        return pl.ds(pl.multiple_of(s * share, share), share)
+
+    def send(src, dst, ss, rs, where):
+        copy = pltpu.make_async_remote_copy(
+            src_ref=src, dst_ref=dst, send_sem=ss, recv_sem=rs, device_id=where,
+            device_id_type=MESH,
+        )
+        copy.start()
+        return copy
+
+    def peer(j):
+        return lax.rem(r + j, n_gr)
+
+    local_w = pltpu.make_async_copy(wt.at[:, cols(r)], wq, loc.at[0])
+    local_f = pltpu.make_async_copy(feat, fa.at[r], loc.at[1])
+    local_v = pltpu.make_async_copy(vals.at[0], vv, loc.at[2])
+    local_c = pltpu.make_async_copy(cot.at[:, cols(r)], cq.at[r], loc.at[3])
+    local_all = pltpu.make_async_copy(wt, wv, loc.at[4])
+    for copy in (local_v, local_f, local_w, local_c, local_all):
+        copy.start()
+
+    barrier = pltpu.get_barrier_semaphore()
+    for j in range(1, n_gr):
+        pl.semaphore_signal(barrier, inc=1, device_id={"gr": peer(j)}, device_id_type=MESH)
+    pl.semaphore_signal(barrier, inc=1, device_id={"gc": z * 2 + 1 - x}, device_id_type=MESH)
+    for k in range(1, n_z):
+        pl.semaphore_signal(
+            barrier, inc=1, device_id={"gc": lax.rem(z + k, n_z) * 2 + x}, device_id_type=MESH
+        )
+    pl.semaphore_wait(barrier, n_gr - 1 + n_z)
+
+    sent = []
+    f_far = [
+        send(feat, fa.at[r], f_s.at[d], f_r.at[d], {"gr": lax.rem(chip + d, chips) * 2 + core})
+        for d in range(1, chips)
+    ]
+    f_mate = send(feat, fa.at[r], f_s.at[0], f_r.at[0], {"gr": mate})
+
+    local_v.wait()
+    for m in range(n_gr):
+        tile = jnp.zeros((rows, rows), f32)
+        for k in range(vv.shape[0]):
+            hit = jnp.logical_and(k < count[0], (codes[0, k] % (n_gr * n_gc)) // n_gc == m)
+            tile = tile + vv[k].astype(f32) * jnp.where(hit, 1.0, 0.0)
+        aa[rowsof(r), m * rows:(m + 1) * rows] = tile.astype(bf16)
+    a_far = [
+        send(aa.at[rowsof(r)], aa.at[rowsof(r)], a_s.at[d], a_r.at[d],
+             {"gr": lax.rem(chip + d, chips) * 2 + core})
+        for d in range(1, chips)
+    ]
+    a_mate = send(aa.at[rowsof(r)], aa.at[rowsof(r)], a_s.at[0], a_r.at[0], {"gr": mate})
+
+    def project(s):
+        block = fa[s]
+        pj[rowsof(s), :] = jnp.dot(block, wq[...], preferred_element_type=f32).astype(bf16)
+        ft[:, rowsof(s)] = block.T
+
+    local_f.wait()
+    local_w.wait()
+    project(r)
+    f_mate.wait_recv()
+    project(mate)
+    f_next = []
+    for d in range(1, chips):
+        s = lax.rem(chip + chips - d, chips) * 2 + core
+        f_far[d - 1].wait_recv()
+        f_next.append(send(fa.at[s], fa.at[s], g_s.at[d], g_r.at[d], {"gr": mate}))
+    a_next = []
+    c_all = [
+        send(cot.at[:, cols(peer(j))], cq.at[r], c_s.at[j], c_r.at[j], {"gr": peer(j)})
+        for j in range(1, n_gr)
+    ]
+    for d in range(1, chips):
+        project(lax.rem(chip + chips - d, chips) * 2 + core)
+    for d in range(1, chips):
+        s = lax.rem(chip + chips - d, chips) * 2 + core
+        a_far[d - 1].wait_recv()
+        a_next.append(send(aa.at[rowsof(s)], aa.at[rowsof(s)], b_s.at[d], b_r.at[d], {"gr": mate}))
+    for d in range(1, chips):
+        f_next[d - 1].wait_recv()
+        project(lax.rem(chip + chips - d, chips) * 2 + 1 - core)
+    a_mate.wait_recv()
+    for copy in a_next:
+        copy.wait_recv()
+    local_c.wait()
+    for copy in c_all:
+        copy.wait_recv()
+
+    for i in range(n_gr):
+        summed = jnp.dot(aa[i * rows:(i + 1) * rows, :], pj[...], preferred_element_type=f32)
+        sigmoid = jax.nn.sigmoid(summed)
+        ob[i] = (summed * sigmoid).astype(bf16)
+        slope = cq[i].astype(f32) * sigmoid * (1.0 + summed * (1.0 - sigmoid))
+        cq[i] = slope.astype(bf16)
+    slope_all = cq[...].reshape(n_gr * rows, share)
+    for i in range(n_gr):
+        bq[i] = jnp.dot(
+            aa[i * rows:(i + 1) * rows, :], slope_all, preferred_element_type=f32
+        ).astype(bf16)
+    back = bq[...].reshape(n_gr * rows, share)
+
+    depth = width // n_gc
+
+    def grad_rows(zz, xx):
+        at = pl.ds(pl.multiple_of((zz * 2 + xx) * depth, depth), depth)
+        return jnp.dot(ft[at, :], back, preferred_element_type=f32)
+
+    order = [k % n_z for k in range(1, n_z + 1)]
+    x_all = {}
+    for k in order:
+        xs[k] = grad_rows(lax.rem(z + k, n_z), 1 - x).astype(bf16)
+        x_all[k] = send(xs.at[k], xr.at[k], x_s.at[k], x_r.at[k], {"gc": z * 2 + 1 - x})
+    k_all = [
+        send(bq.at[peer(j)], br.at[:, cols(r)], k_s.at[j], k_r.at[j], {"gr": peer(j)})
+        for j in range(1, n_gr)
+    ]
+    o_all = [
+        send(ob.at[peer(j)], out_o.at[:, cols(r)], o_s.at[j], o_r.at[j], {"gr": peer(j)})
+        for j in range(1, n_gr)
+    ]
+    own_o = pltpu.make_async_copy(ob.at[r], out_o.at[:, cols(r)], loc.at[5])
+    own_o.start()
+    br[:, cols(r)] = bq[r]
+    for k in order:
+        ac[k] = grad_rows(lax.rem(z + k, n_z), x)
+    z_all = {}
+    for k in order:
+        x_all[k].wait_recv()
+        if k > 0:
+            zs[k] = (ac[k] + xr[k].astype(f32)).astype(bf16)
+            z_all[k] = send(
+                zs.at[k], zr.at[k], z_s.at[k], z_r.at[k], {"gc": lax.rem(z + k, n_z) * 2 + x}
+            )
+    for copy in k_all:
+        copy.wait_recv()
+    local_all.wait()
+    step = 256
+    for i in range(width // step):
+        iv[:, i * step:(i + 1) * step] = lax.dot_general(
+            br[...], wv[i * step:(i + 1) * step, :], (((1,), (1,)), ((), ())),
+            preferred_element_type=f32,
+        )
+    own_i = pltpu.make_async_copy(iv, ig_o, loc.at[6])
+    own_i.start()
+    total = ac[0] + xr[0].astype(f32)
+    for k in range(1, n_z):
+        z_all[k].wait_recv()
+        total = total + zr[k].astype(f32)
+    wb[...] = (total * scale).astype(bf16)
+    w_all = [
+        send(wb, wg_o.at[:, cols(r)], w_s.at[j], w_r.at[j], {"gr": peer(j)})
+        for j in range(1, n_gr)
+    ]
+    own_w = pltpu.make_async_copy(wb, wg_o.at[:, cols(r)], loc.at[7])
+    own_w.start()
+    for copy in [f_mate, a_mate] + f_far + a_far + f_next + a_next + c_all:
+        copy.wait_send()
+    for copy in list(x_all.values()) + list(z_all.values()) + k_all:
+        copy.wait_send()
+    for copy in o_all + w_all:
+        copy.wait()
+    own_o.wait()
+    own_i.wait()
+    own_w.wait()
+
+
+def by_columns(features, weight, cotangent, block_values, block_codes, block_count):
+    n_gr, n_gc = lax.axis_size("gr"), lax.axis_size("gc")
+    rows, width = features.shape
+    slots = block_values.shape[1]
+    share, depth, n_z = width // n_gr, width // n_gc, n_gc // 2
+    f32, bf16 = jnp.float32, jnp.bfloat16
+    dma = pltpu.SemaphoreType.DMA
+    everywhere = pl.BlockSpec(memory_space=pl.ANY)
+    scalars = pl.BlockSpec(memory_space=pltpu.SMEM)
+    chips = n_gr // 2
+    out, input_grad, weight_grad = pl.pallas_call(
+        functools.partial(layer_kernel, n_gr, n_gc, (rows * n_gr * n_gc) ** (-0.5)),
+        out_shape=(
+            jax.ShapeDtypeStruct((rows, width), bf16),
+            jax.ShapeDtypeStruct((rows, width), f32),
+            jax.ShapeDtypeStruct((depth, width), bf16),
+        ),
+        in_specs=[everywhere] * 4 + [scalars] * 2,
+        out_specs=(everywhere,) * 3,
+        scratch_shapes=[
+            pltpu.VMEM((n_gr, rows, width), bf16),
+            pltpu.VMEM((width, n_gr * rows), bf16),
+            pltpu.VMEM((width, share), bf16),
+            pltpu.VMEM((width, width), bf16),
+            pltpu.VMEM((slots, rows, rows), bf16),
+            pltpu.VMEM((n_gr * rows, n_gr * rows), bf16),
+            pltpu.VMEM((n_gr * rows, share), bf16),
+            pltpu.VMEM((n_gr, rows, share), bf16),
+            pltpu.VMEM((n_gr, rows, share), bf16),
+            pltpu.VMEM((n_gr, rows, share), bf16),
+            pltpu.VMEM((rows, width), bf16),
+            pltpu.VMEM((rows, width), f32),
+            pltpu.VMEM((n_z, depth, share), bf16),
+            pltpu.VMEM((n_z, depth, share), bf16),
+            pltpu.VMEM((n_z, depth, share), f32),
+            pltpu.VMEM((n_z, depth, share), bf16),
+            pltpu.VMEM((n_z, depth, share), bf16),
+            pltpu.VMEM((depth, share), bf16),
+            dma((8,)),
+        ]
+        + [dma((chips,))] * 8
+        + [dma((n_gr,))] * 6
+        + [dma((n_z,))] * 4
+        + [dma((n_gr,))] * 2,
+        compiler_params=pltpu.CompilerParams(
+            collective_id=0, has_side_effects=True, vmem_limit_bytes=32 * 1024 * 1024
+        ),
+        cost_estimate=pl.CostEstimate(
+            flops=2 * rows * width * (3 * width + 2 * n_gr * rows),
+            bytes_accessed=6 * width * width,
+            transcendentals=rows * width,
+        ),
+    )(features, weight, cotangent, block_values, block_codes, block_count)
+    return (out.astype(f32), input_grad, weight_grad.astype(f32))
+
+
+def local(features, weight, cotangent, block_values, block_codes, block_count):
+    n_gr, n_gc = lax.axis_size("gr"), lax.axis_size("gc")
+    rows, width = features.shape
+    whole = width % (128 * n_gr) == 0 and width % (16 * n_gc) == 0
+    even = n_gr % 2 == 0 and n_gc % 2 == 0
+    take = by_columns if whole and even and rows == block_values.shape[-1] else by_rows
+    return take(features, weight, cotangent, block_values, block_codes, block_count)
+
+
 def solution(mesh):
     in_specs = (
         P(("gr", "gc"), None),

time: 187 us -> 44.2 us (0.24); the launches traced: 185 us -> 44 us
  waiting for transfers between devices: 156 us -> 0 us
  Pallas kernels: 0 us -> 35.1 us
  between operations: 14.5 us -> 1.3 us
  matrix products: 10.7 us -> 0 us
  local copies, waits for them, and re-layouts: 3.56 us -> 5.83 us
    reduce_scatter x1 -> x0, waiting for transfers between devices: 88.2 us -> none  [local(): lax.psum_scatter(partial_grad, 'gc', scatter_dimension=0, tiled=True)]
    all_gather x2 -> x0, waiting for transfers between devices: 35.2 us -> none  [aggregate(): portion = lax.all_gather(source, 'gr', axis=0, tiled=True)]
    pallas_call x0 -> x1, Pallas kernels: none -> 35.1 us  [by_columns(): pl.pallas_call(functools.partial(layer_kernel, n_gr, n_gc, (rows * n_gr *...]
    psum x1 -> x0, waiting for transfers between devices: 32.1 us -> none  [local(): weight_grad = lax.psum(row_share, 'gr')]
    dot_general x6 -> x0, matrix products: 10.7 us -> none  [the longest x2 4.13 us: aggregate(): return jnp.dot(tile, portion, preferred_element_type=jnp.float32)]
    unnamed x11, local copies, waits for them, and re-layouts: 3.56 us -> 5.83 us
  transfers between devices with their start and end apart: 4 -> 0, of which waited for: 4 -> 0; matrix products, arithmetic and copies ran while one was open for 1% -> 0% of each run, Pallas kernels for 0% -> 0%
where the time goes in v1:
time: 44.2 us; the launch traced here: 44 us
  Pallas kernels  35.1 us (79%)
  local copies, waits for them, and re-layouts  5.83 us (13%)
  other arithmetic  1.68 us (4%)
  between operations  1.3 us (3%)
    pallas_call x1, Pallas kernels, by_columns(): pl.pallas_call(functools.partial(layer_kernel, n_gr, n_gc, (rows * n_gr *...  35.1 us
    unnamed x11, local copies, waits for them, and re-layouts  5.83 us
    convert_element_type x2, other arithmetic, by_columns(): return (out.astype(f32), input_grad, weight_grad.astype(f32))  1.68 us

profile of v1, /device:TPU:1, one launch (start us, length us, event | category | flops | bytes accessed | tf_op | source)
XLA Modules:
  0.0 44.0 jit_solution(7364308092684840984)
XLA Ops:
  1.3 0.0 copy-start
  1.3 1.6 %copy-done = bf16[1024,1024]{1,0:T(8,128)(2,1)S(1)} copy-done((bf16[1024,1024]{1,0:T(8,128)(2,1)S(1)}, bf16[1024,1024]{1,0:T(8,128)(2,1)}, u32[]{:S(2)}) %copy-start) | copy-done | bytes 2097176
  2.9 0.0 copy-start.1
  2.9 0.9 %copy-done.1 = bf16[128,1024]{1,0:T(8,128)(2,1)S(1)} copy-done((bf16[128,1024]{1,0:T(8,128)(2,1)S(1)}, bf16[128,1024]{1,0:T(8,128)(2,1)}, u32[]{:S(2)}) %copy-start.1) | copy-done | bytes 262168
  3.8 0.0 copy-start.2
  3.8 0.9 %copy-done.2 = bf16[128,1024]{1,0:T(8,128)(2,1)S(1)} copy-done((bf16[128,1024]{1,0:T(8,128)(2,1)S(1)}, bf16[128,1024]{1,0:T(8,128)(2,1)}, u32[]{:S(2)}) %copy-start.2) | copy-done | bytes 262168
  4.8 0.0 copy-start.3
  4.8 0.9 %copy-done.3 = bf16[1,4,128,128]{3,2,1,0:T(8,128)(2,1)S(1)} copy-done((bf16[1,4,128,128]{3,2,1,0:T(8,128)(2,1)S(1)}, bf16[1,4,128,128]{3,2,1,0:T(8,128)(2,1)}, u32[]{:S(2)}) %copy-start.3) | copy-done | bytes 131096
  5.7 0.0 copy-start.4
  5.7 0.7 %copy-done.4 = s32[1,4]{1,0:T(1,128)S(1)} copy-done((s32[1,4]{1,0:T(1,128)S(1)}, s32[1,4]{1,0:T(1,128)}, u32[]{:S(2)}) %copy-start.4) | copy-done | bytes 40
  6.3 35.1 %shard_map.85 = (bf16[128,1024]{1,0:T(8,128)(2,1)S(1)}, f32[128,1024]{1,0:T(8,128)S(1)}, bf16[128,1024]{1,0:T(8,128)(2,1)S(1)}) custom-call(bf16[128,1024]{1,0:T(8,128)(2,1)S(1)} %copy-done.1, bf16[1024,1024]{1,0:T(8,128)(2,1)S(1)} %copy-done, bf16[128,1024]{1,0:T(8,128)(2,1)S(1)} %copy-done.2, bf16[1,4,128,128]{3,2,1,0:T(8,128)(2,1)S(1)} %copy-done.3, ...), custom_call_target="tpu_custom_call" | custom-call | flops 1073741824 | bytes 6291456 | tf_op jit(solution)/shard_map/pallas_call | solution.py:272
  41.5 0.8 %convert_element_type.6 = f32[128,1024]{1,0:T(8,128)} convert(bf16[128,1024]{1,0:T(8,128)(2,1)S(1)} %get-tuple-element.6) | non-fusion elementwise | flops 131072 | bytes 786432 | tf_op jit(solution)/shard_map/convert_element_type | solution.py:315
  42.3 0.8 %convert_element_type.7 = f32[128,1024]{1,0:T(8,128)} convert(bf16[128,1024]{1,0:T(8,128)(2,1)S(1)} %get-tuple-element.8) | non-fusion elementwise | flops 131072 | bytes 786432 | tf_op jit(solution)/shard_map/convert_element_type | solution.py:315
  43.2 0.8 %copy.11 = f32[128,1024]{1,0:T(8,128)} copy(f32[128,1024]{1,0:T(8,128)S(1)} %get-tuple-element.13) | data formatting | bytes 1048576
Async XLA Ops:
  1.3 1.6 %copy-start = (bf16[1024,1024]{1,0:T(8,128)(2,1)S(1)}, bf16[1024,1024]{1,0:T(8,128)(2,1)}, u32[]{:S(2)}) copy-start(bf16[1024,1024]{1,0:T(8,128)(2,1)} %wt.1) | copy-start | bytes 6291460
  2.9 0.9 %copy-start.1 = (bf16[128,1024]{1,0:T(8,128)(2,1)S(1)}, bf16[128,1024]{1,0:T(8,128)(2,1)}, u32[]{:S(2)}) copy-start(bf16[128,1024]{1,0:T(8,128)(2,1)} %feat.1) | copy-start | bytes 786436
  3.8 0.9 %copy-start.2 = (bf16[128,1024]{1,0:T(8,128)(2,1)S(1)}, bf16[128,1024]{1,0:T(8,128)(2,1)}, u32[]{:S(2)}) copy-start(bf16[128,1024]{1,0:T(8,128)(2,1)} %cot.1) | copy-start | bytes 786436
  4.8 0.9 %copy-start.3 = (bf16[1,4,128,128]{3,2,1,0:T(8,128)(2,1)S(1)}, bf16[1,4,128,128]{3,2,1,0:T(8,128)(2,1)}, u32[]{:S(2)}) copy-start(bf16[1,4,128,128]{3,2,1,0:T(8,128)(2,1)} %vals.1) | copy-start | bytes 393220
  5.7 0.7 %copy-start.4 = (s32[1,4]{1,0:T(1,128)S(1)}, s32[1,4]{1,0:T(1,128)}, u32[]{:S(2)}) copy-start(s32[1,4]{1,0:T(1,128)} %codes.1) | copy-start | bytes 52
